TPU v7x, 512 devices: a whole 4x4x16 slice. The times are simulated.
512 devices in a mesh: attn: 32 (over z, core), ffn: 4 (over x), rep: 4 (over y).
Axes of the slice: x: 4, y: 4, z: 16, core: 2. Of those that a mesh axis runs over, the one named last changes fastest.
Arguments:
- queries: bfloat16 [4, 128, 16384], P('rep', 'attn', 'ffn'), may hold values from -6 to 6
- keys: bfloat16 [4, 128, 256, 256], P('rep', 'attn'), may hold values from -6 to 6
- values: bfloat16 [4, 128, 256, 256], P('rep', 'attn'), may hold values from -6 to 6
- lengths: int32 [4, 128], P('rep', 'attn'), may hold values from 2 to 256
- out_proj: bfloat16 [7168, 16384], P('attn', 'ffn'), may hold values from -0.046875 to 0.046875
- residual: bfloat16 [4, 128, 7168], P('rep', 'ffn', 'attn'), may hold values from -6 to 6
- norm_gain: float32 [7168], P('attn'), may hold values from 0.1 to 1.9
- expert_ids: int32 [4, 128, 3], P('rep', 'ffn'), may hold values from 0 to 7, all different within a row; in each aligned block of 32 rows (0 to 31, 32 to 63, ..., all dimensions but the last counted through in order) at most 14 rows name the same one
- gate_weights: float32 [4, 128, 3], P('rep', 'ffn'), may hold values from 0.1 to 1
- w_gate: bfloat16 [8, 7168, 2560], P('ffn', 'attn', 'rep'), may hold values from -0.0625 to 0.0625
- w_up: bfloat16 [8, 7168, 2560], P('ffn', 'attn', 'rep'), may hold values from -0.0625 to 0.0625
- w_down: bfloat16 [8, 7168, 2560], P('ffn', 'attn', 'rep'), may hold values from -0.125 to 0.125
Outputs:
- mixed: float32 [4, 128, 7168], P('rep', 'ffn', 'attn')
Inputs may be any that keep to these rules, and one draw needn't show every extreme that they name: `expert_ids`: each row names 3 different experts. In each aligned block of 32 rows of one batch, no expert is named by more than 14 rows, a bound that some block reaches.
All inputs are finite; a program needn't handle non-finite values.
Results may differ from a plain program's by a relative error of at most 0.007.
Values may be sent and summed in bfloat16 or wider, within the bound.
A program may use at most 64 MiB of HBM per device.

v0:
```python
import jax
import jax.numpy as jnp
from jax import lax
from jax.sharding import PartitionSpec as P


def per_device(
    queries,
    keys,
    values,
    lengths,
    out_proj,
    residual,
    norm_gain,
    expert_ids,
    gate_weights,
    w_gate,
    w_up,
    w_down,
):
    requests = queries.shape[1]
    head_dim = keys.shape[3]
    local_heads = queries.shape[2] // head_dim
    context = keys.shape[2]
    query_heads = queries[0].reshape(requests, local_heads, head_dim)
    scores = jnp.einsum(
        "rhd,rtd->rht", query_heads, keys[0], preferred_element_type=jnp.float32
    ) * head_dim ** (-0.5)
    position = jnp.arange(context, dtype=jnp.int32)
    live = position[None, None, :] < lengths[0][:, None, None]
    scores = jnp.where(live, scores, jnp.float32(-1e30))
    probs = jax.nn.softmax(scores, axis=-1).astype(jnp.bfloat16)
    attended = jnp.einsum("rht,rtd->rhd", probs, values[0], preferred_element_type=jnp.float32)
    attended = attended.astype(jnp.bfloat16).reshape(1, requests, local_heads * head_dim)
    partial_rows = lax.dot_general(
        lax.all_gather(attended, "attn", axis=1, tiled=True)[0],
        out_proj,
        (((1,), (1,)), ((), ())),
        preferred_element_type=jnp.float32,
    )
    share_rows = lax.psum_scatter(partial_rows, "ffn", scatter_dimension=0, tiled=True)
    hidden = residual[0].astype(jnp.float32) + share_rows
    hidden_bf = hidden.astype(jnp.bfloat16)
    n_ffn = lax.axis_size("ffn")
    n_rep = lax.axis_size("rep")
    local_experts = w_gate.shape[0]
    n_experts = local_experts * n_ffn
    width_part = hidden.shape[1]
    quarter = expert_ids.shape[1]
    top_count = expert_ids.shape[2]
    capacity = min(quarter, 14)
    routes = expert_ids[0]
    gate_share = gate_weights[0]
    expert_range = jnp.arange(n_experts, dtype=jnp.int32)
    hits = (routes[:, :, None] == expert_range[None, None, :]).astype(jnp.int32)
    flat_hits = hits.reshape(quarter * top_count, n_experts)
    before = jnp.cumsum(flat_hits, axis=0) - flat_hits
    slot_index = jnp.sum(before * flat_hits, axis=1).reshape(quarter, top_count)
    slot_range = jnp.arange(capacity, dtype=jnp.int32)
    match_map = (routes[None, None, :, :] == expert_range[:, None, None, None]) & (
        slot_index[None, None, :, :] == slot_range[None, :, None, None]
    )
    match_map = match_map.astype(jnp.float32)
    select_map = jnp.sum(match_map, axis=3)
    weighted_map = jnp.sum(match_map * gate_share[None, None, :, :], axis=3)
    table = jnp.einsum(
        "ecq,qw->ecw",
        select_map.astype(jnp.bfloat16),
        hidden_bf,
        preferred_element_type=jnp.float32,
    )
    table = table.astype(jnp.bfloat16).reshape(n_ffn, local_experts, capacity, width_part)
    everything = lax.all_gather(table[None], ("ffn", "rep"), axis=0, tiled=True)
    inbox = lax.dynamic_index_in_dim(everything, lax.axis_index("ffn"), 1, keepdims=False)
    inbox = inbox.reshape(n_ffn, n_rep, local_experts, capacity, width_part)
    slot_rows = jnp.transpose(inbox, (2, 0, 1, 3, 4)).reshape(local_experts, -1, width_part)
    slot_float = slot_rows.astype(jnp.float32)
    squares = jnp.sum(slot_float * slot_float, axis=-1)
    normed = (slot_float * norm_gain).astype(jnp.bfloat16)
    gate_part = jnp.einsum("esw,ewf->esf", normed, w_gate, preferred_element_type=jnp.float32)
    up_part = jnp.einsum("esw,ewf->esf", normed, w_up, preferred_element_type=jnp.float32)
    model_width = norm_gain.shape[0] * lax.axis_size("attn")
    gate_part, up_part, squares = lax.psum((gate_part, up_part, squares), "attn")
    rinv = lax.rsqrt(squares / model_width + 1e-06)[..., None]
    activated = (jax.nn.silu(gate_part * rinv) * (up_part * rinv)).astype(jnp.bfloat16)
    expert_out = jnp.einsum("esf,ewf->esw", activated, w_down, preferred_element_type=jnp.float32)
    expert_out = expert_out.reshape(local_experts, n_ffn, n_rep, capacity, width_part)
    expert_out = jnp.transpose(expert_out, (1, 2, 0, 3, 4))
    owner = (jnp.arange(n_ffn, dtype=jnp.int32) == lax.axis_index("ffn")).astype(jnp.float32)
    padded = expert_out[:, :, None] * owner[None, None, :, None, None, None]
    padded = padded.reshape(n_ffn * n_rep, n_ffn, local_experts, capacity, width_part)
    returned = lax.psum_scatter(padded, ("ffn", "rep"), scatter_dimension=0, tiled=True)
    returned = returned.reshape(n_experts, capacity, width_part)
    moe_out = jnp.einsum("ecq,ecw->qw", weighted_map, returned, precision=lax.Precision.HIGHEST)
    return (hidden + moe_out)[None]


def solution(mesh):
    in_specs = (
        P("rep", "attn", "ffn"),
        P("rep", "attn", None, None),
        P("rep", "attn", None, None),
        P("rep", "attn"),
        P("attn", "ffn"),
        P("rep", "ffn", "attn"),
        P("attn"),
        P("rep", "ffn", None),
        P("rep", "ffn", None),
        P("ffn", "attn", "rep"),
        P("ffn", "attn", "rep"),
        P("ffn", "attn", "rep"),
    )
    out_specs = P("rep", "ffn", "attn")
    return jax.shard_map(
        per_device, mesh=mesh, in_specs=in_specs, out_specs=out_specs, check_vma=False
    )
```

profile of v0, /device:TPU:6, one launch (start us, length us, event | category | flops | bytes accessed | tf_op | source)
XLA Modules:
  0.0 493.4 jit_solution(7326458006173938262)
XLA Ops:
  6.5 0.9 iota_compare_fusion.3
  7.4 1.3 fusion.3
  8.7 0.2 fusion.30
  8.9 1.3 convolution_convert_fusion.1
  10.2 0.6 reshape.90
  11.0 0.1 eq.70
  11.2 0.1 reduce_window_sum.11
  11.3 0.2 select_reduce_fusion
  11.5 0.1 eq.74
  11.8 75.5 %all-gather.2.cloned.1.call-done = bf16[1,128,4096]{2,0,1:T(2,128)(2,1)} async-done(((bf16[1,4,4096]{2,0,1:T(2,128)(2,1)}), bf16[1,128,4096]{2,0,1:T(2,128)(2,1)}) %all-gather.2.cloned.1.call-update) | async-done | bytes 1048592 | tf_op jit(solution)/shard_map/all_gather | solution.py:36
  87.2 3.7 fusion.6
  91.1 23.8 %reduce-scatter.2.cloned.1.call-done = f32[32,224]{1,0:T(8,128)} async-done(((f32[128,224]{1,0:T(8,128)}), f32[32,224]{1,0:T(8,128)}) %reduce-scatter.2.cloned.1.call-update) | async-done | bytes 28688 | tf_op jit(solution)/shard_map/reduce_scatter | solution.py:41
  114.9 0.9 convolution_convert_fusion
  115.9 23.5 %all_gather.7 = bf16[16,4,2,14,224]{4,1,3,2,0:T(4,128)(2,1)S(1)} all-gather(bf16[1,4,2,14,224]{4,1,3,2,0:T(4,128)(2,1)S(1)} %copy.70), channel_id=1, replica_groups=mesh['attn'=32,'ffn'=4,'rep'=4] {'ffn','rep'}, dimensions={0}, use_global_device_ids=true | all-gather | bytes 852992 | tf_op jit(solution)/shard_map/all_gather | solution.py:73
  139.4 0.5 constant_dynamic-slice_fusion.1
  139.9 0.1 copy_convert_fusion
  140.0 0.4 copy.72
  140.4 0.6 copy-done.1
  140.9 1.3 fusion.15
  142.3 1.3 fusion.17
  143.7 0.2 multiply_reduce_fusion
  143.9 0.1 copy.82
  144.0 0.1 reduce_sum.58
  144.1 46.6 %psum.22 = f32[2,224]{1,0:T(2,128)S(1)} all-reduce(f32[2,224]{1,0:T(2,128)S(1)} %reduce_sum.58), channel_id=1, replica_groups=mesh['attn'=32,'ffn'=4,'rep'=4] {'attn'}, use_global_device_ids=true, to_apply=%region_9.10 | all-reduce | flops 448 | bytes 3584 | tf_op jit(solution)/shard_map/psum | solution.py:83
  190.7 169.2 %all-reduce.7.cloned.1.call-done = (f32[2,224,640]{2,1,0:T(8,128)}, f32[2,224,640]{2,1,0:T(8,128)}) async-done(((f32[2,224,640]{2,1,0:T(8,128)}, f32[2,224,640]{2,1,0:T(8,128)}), (f32[2,224,640]{2,1,0:T(8,128)}, f32[2,224,640]{2,1,0:T(8,128)})) %all-reduce.7.cloned.1.call-update) | async-done | bytes 2293776 | tf_op jit(solution)/shard_map/psum | solution.py:83
  359.9 2.1 fusion.9
  362.0 0.4 copy.76
  362.4 1.7 broadcast_multiply_fusion
  364.2 1.3 dynamic-slice
  365.4 118.8 %all-reduce.5.cloned.1.call-done = f32[16,4,2,14,224]{4,1,3,2,0:T(4,128)} async-done(((f32[16,4,2,14,224]{4,1,3,2,0:T(4,128)}), f32[16,4,2,14,224]{4,1,3,2,0:T(4,128)}) %all-reduce.5.cloned.1.call-update) | async-done | bytes 1605648
  484.2 1.6 constant_dynamic-slice_fusion
  486.0 0.9 fusion.5
  (40 shorter events, 0.8 us)
Async XLA Ops:
  6.5 80.7 %copy-start = (bf16[224,4096]{1,0:T(8,128)(2,1)S(1)}, bf16[224,4096]{1,0:T(8,128)(2,1)}, u32[]{:S(2)}) copy-start(bf16[224,4096]{1,0:T(8,128)(2,1)} %param.16) | copy-start | bytes 5505028
  6.5 4.4 copy-start.5
  6.5 80.7 %all-gather.2.cloned.1.call-start = ((), (), s32[]{:S(2)}) async-start(), calls=%async_computation.1 | async-start | bytes 2162688 | tf_op jit(solution)/shard_map/all_gather | solution.py:36
  10.9 104.0 %reduce-scatter.2.cloned.1.call-start = ((), (), s32[]{:S(2)}) async-start(), calls=%async_computation.2 | async-start | bytes 163840 | tf_op jit(solution)/shard_map/reduce_scatter | solution.py:41
  11.7 79.3 %copy-start.7 = (f32[1,32,3]{1,0,2:T(1,128)S(1)}, f32[1,32,3]{1,0,2:T(1,128)}, u32[]{:S(2)}) copy-start(f32[1,32,3]{1,0,2:T(1,128)} %param.20) | copy-start | bytes 1156
  11.8 103.1 %copy-start.4 = (bf16[1,32,224]{2,1,0:T(8,128)(2,1)S(1)}, bf16[1,32,224]{2,1,0:T(8,128)(2,1)}, u32[]{:S(2)}) copy-start(bf16[1,32,224]{2,1,0:T(8,128)(2,1)} %param.17) | copy-start | bytes 43012
  90.9 268.9 %all-reduce.7.cloned.1.call-start = ((), (), s32[]{:S(2)}) async-start(), calls=%async_computation.4 | async-start | bytes 4587520 | tf_op jit(solution)/shard_map/psum | solution.py:83
  139.9 1.1 copy-start.1
  139.9 1.1 copy-start.6
  140.4 1.9 copy-start.2
  143.6 216.2 %copy-start.8 = (bf16[2,224,640]{2,1,0:T(8,128)(2,1)S(1)}, bf16[2,224,640]{2,1,0:T(8,128)(2,1)}, u32[]{:S(2)}) copy-start(bf16[2,224,640]{2,1,0:T(8,128)(2,1)} %param.23) | copy-start | bytes 1720324
  143.7 340.6 %all-reduce.5.cloned.1.call-start = ((), (), s32[]{:S(2)}) async-start(), calls=%async_computation.3 | async-start | bytes 3670016
  364.1 121.8 %copy-start.3 = (f32[32,224]{1,0:T(8,128)S(1)}, f32[32,224]{1,0:T(8,128)}, u32[]{:S(2)}) copy-start(f32[32,224]{1,0:T(8,128)} %reduce-scatter.2.cloned.1.call-done) | copy-start | bytes 86020
Sparse Core Ops, SparseCore 0:
  11.0 76.2 all-gather.1
  91.1 23.7 reduce-scatter.1
  143.8 216.0 all-reduce.6
  364.3 119.9 all-reduce.4
where the time goes:
time: 494 us; the launch traced here: 493 us
  waiting for transfers between devices  387 us (78%)
  blocking collectives  70.1 us (14%)
  between operations  13.4 us (3%)
  matrix products  12.8 us (3%)
  local copies, waits for them, and re-layouts  6.08 us (1%)
    psum x1, waiting for transfers between devices, per_device(): lax.psum((gate_part, up_part, squares), 'attn')  169 us
    unnamed x5, waiting for transfers between devices  119 us
    all_gather x1, waiting for transfers between devices, per_device(): lax.all_gather(attended, 'attn', axis=1, tiled=True)[0]  75.5 us
    psum x1, blocking collectives, per_device(): lax.psum((gate_part, up_part, squares), 'attn')  46.6 us
    reduce_scatter x1, waiting for transfers between devices, per_device(): lax.psum_scatter(partial_rows, 'ffn', scatter_dimension=0, tiled=True)  23.8 us
    all_gather x1, blocking collectives, per_device(): everything = lax.all_gather(table[None], ('ffn', 'rep'), axis=0, tiled=True)  23.5 us
  transfers between devices with their start and end apart: 4, of which 4 were waited for; matrix products, arithmetic and copies ran while one was open for 1% of the time, Pallas kernels for 0%

commit v1 on v0

v1 whole, which is shorter than its diff:
```python
import functools

import jax
import jax.numpy as jnp
from jax import lax
from jax.experimental import pallas as pl
from jax.experimental.pallas import tpu as pltpu
from jax.sharding import PartitionSpec as P

MESH = pl.DeviceIdType.MESH
BF = jnp.bfloat16
F32 = jnp.float32
NT = (((1,), (1,)), ((), ()))
NN = (((1,), (0,)), ((), ()))

CHIPS = 16
SIDE = 4
W = 224
WP = 256
CAP = 14
SLOT = 16
ROWS = 32
EFF = 640
HD = 256
KH = 2048
D = 7168

PLANE = sorted(
    ((df, dr, dc) for df in range(4) for dr in range(4) for dc in range(2) if df or dr or dc),
    key=lambda o: (-(min(o[0], 4 - o[0]) + min(o[1], 4 - o[1])), o),
)
XCORE = sorted(
    ((df, dc) for df in range(4) for dc in range(2) if df or dc),
    key=lambda o: (-min(o[0], 4 - o[0]), o),
)


def mm(a, b, dims=NN):
    return lax.dot_general(a, b, dims, preferred_element_type=F32)


def kernel(
    q_h, k_h, v_h, len_h, wo_h, res_h, gain_h, ids_h, gw_h, wg_h, wu_h, wd_h,
    out_ref,
    qv, kv, vv, lenv, resv, gainv, idsv, gwv, wo, wg, wu, wd,
    qs, att, xs, xr, ag1, us, rb, pad32, pad1, tok, xb, pb, r1, ra, s2, r2, ag2, eb, rr,
    ld, ss, rs,
):
    a = lax.axis_index("attn")
    f = lax.axis_index("ffn")
    r = lax.axis_index("rep")
    c = lax.rem(a, 2)
    z = lax.div(a, 2)
    sg = 1 - 2 * c

    def zdev(d):
        return {"attn": lax.rem(z + d + CHIPS, CHIPS) * 2 + c}

    def zidx(d):
        return lax.rem(z + d + 2 * CHIPS, CHIPS)

    def pdev(o):
        df, dr, dc = o
        return {
            "attn": z * 2 + lax.rem(c + dc, 2),
            "ffn": lax.rem(f + df, 4),
            "rep": lax.rem(r + dr, 4),
        }

    sib = {"attn": z * 2 + 1 - c}

    loads = []

    def load(src, dst):
        cp = pltpu.make_async_copy(src, dst, ld.at[len(loads)])
        cp.start()
        loads.append(cp)
        return cp

    sent = []

    def send(src, dst, dev):
        k = len(sent)
        cp = pltpu.make_async_remote_copy(
            src_ref=src, dst_ref=dst, send_sem=ss.at[k], recv_sem=rs.at[k],
            device_id=dev, device_id_type=MESH,
        )
        cp.start()
        sent.append(cp)
        return cp

    l_q = load(q_h.at[0], qv)
    l_k = load(k_h.at[0], kv)
    l_v = load(v_h.at[0], vv)
    l_len = load(len_h, lenv)
    l_ids = load(ids_h.at[0], idsv)
    l_gw = load(gw_h.at[0], gwv)
    l_res = load(res_h.at[0], resv)
    l_gain = load(gain_h, gainv)

    barrier = pltpu.get_barrier_semaphore()
    peers = [pdev(o) for o in PLANE] + [zdev(d) for d in (6, -6, 3, -3, 2, -2, 1, -1)]
    for dev in peers:
        pl.semaphore_signal(barrier, inc=1, device_id=dev, device_id_type=MESH)

    half = pl.multiple_of(c * KH, KH)
    other = pl.multiple_of((1 - c) * KH, KH)
    l_wo = load(wo_h.at[:, pl.ds(half, KH)], wo.at[c, pl.ds(0, W)])
    l_wg = load(wg_h.at[c], wg.at[c, pl.ds(0, W)])
    l_wu = load(wu_h.at[c], wu.at[c, pl.ds(0, W)])
    l_wd = load(wd_h.at[c], wd.at[c, pl.ds(0, W)])

    l_q.wait()
    q32 = qv[...].astype(F32)
    for i in range(4):
        for h in range(16):
            qs[i * 16 + h : i * 16 + h + 1, :] = q32[i : i + 1, h * HD : (h + 1) * HD]
    l_k.wait()
    l_len.wait()
    l_v.wait()
    position = lax.broadcasted_iota(jnp.int32, (16, HD), 1)
    for i in range(4):
        s = mm(qs[i * 16 : (i + 1) * 16, :].astype(BF), kv[i], NT) * (HD**-0.5)
        s = jnp.where(position < lenv[0:1, i : i + 1], s, F32(-1e30))
        e = jnp.exp(s - jnp.max(s, axis=1, keepdims=True))
        p = (e / jnp.sum(e, axis=1, keepdims=True)).astype(BF)
        o = mm(p, vv[i])
        for h in range(16):
            hh, hg, j = h // 8, (h % 8) // 4, h % 4
            for k in range(2):
                row = hg * 8 + k * 4 + i
                att[hh, row : row + 1, j * HD : (j + 1) * HD] = o[h : h + 1, :]
    rowi = lax.broadcasted_iota(jnp.int32, (16, 1024), 0)
    mine = lax.rem(lax.div(rowi, 4), 2) == c
    xs[...] = jnp.where(mine, att[1 - c], 0.0).astype(BF)

    pl.semaphore_wait(barrier, len(peers))
    x_cp = send(xs, xr, sib)
    x_wo = send(wo_h.at[:, pl.ds(other, KH)], wo.at[c, pl.ds(0, W)], sib)
    x_wg = send(wg_h.at[1 - c], wg.at[c, pl.ds(0, W)], sib)
    x_wu = send(wu_h.at[1 - c], wu.at[c, pl.ds(0, W)], sib)
    x_wd = send(wd_h.at[1 - c], wd.at[c, pl.ds(0, W)], sib)

    def gather_z(buf):
        own = buf.at[z]
        first = {d: send(own, own, zdev(d)) for d in (6, -6, 3, -3, 1, -1)}
        rest = []
        first[6].wait_recv()
        far = buf.at[zidx(-6)]
        rest += [send(far, far, zdev(1)), send(far, far, zdev(-1))]
        first[-6].wait_recv()
        far = buf.at[zidx(6)]
        rest += [send(far, far, zdev(-1)), send(far, far, zdev(1))]
        far = buf.at[zidx(-6 * sg)]
        rest += [send(far, far, zdev(2 * sg))]
        first[3].wait_recv()
        far = buf.at[zidx(-3)]
        rest += [send(far, far, zdev(1)), send(far, far, zdev(-1))]
        first[-3].wait_recv()
        far = buf.at[zidx(3)]
        rest += [send(far, far, zdev(-1)), send(far, far, zdev(1))]
        return [first[1], first[-1]] + rest

    x_cp.wait_recv()
    ag1[z] = jnp.where(mine, att[c], 0.0).astype(BF) + xr[...]
    pending = gather_z(ag1)

    for buf in (wo, wg, wu, wd):
        buf[:, W:WP, :] = jnp.zeros((2, WP - W, buf.shape[2]), BF)
    l_res.wait()
    l_gain.wait()
    l_ids.wait()
    l_gw.wait()
    pad32[...] = jnp.zeros((ROWS, WP), F32)
    pad32[:, 0:W] = resv[...].astype(F32)
    pad1[...] = jnp.zeros((1, WP), F32)
    pad1[:, 0:W] = gainv[...]
    lane = lax.broadcasted_iota(jnp.int32, (ROWS, 128), 1)
    ids = idsv[...]
    gws = gwv[...]
    hits = jnp.zeros((ROWS, 128), F32)
    share = jnp.zeros((ROWS, 128), F32)
    for k in range(3):
        same = ids[:, k : k + 1] == lax.div(lane, SLOT)
        hits = hits + jnp.where(same, 1.0, 0.0)
        share = share + jnp.where(same, gws[:, k : k + 1], 0.0)
    lower = lax.broadcasted_iota(jnp.int32, (ROWS, ROWS), 0) > lax.broadcasted_iota(
        jnp.int32, (ROWS, ROWS), 1
    )
    before = mm(jnp.where(lower, 1.0, 0.0).astype(BF), hits.astype(BF))
    placed = before == lax.rem(lane, SLOT).astype(F32)
    pick_t = jnp.where(placed, hits, 0.0).astype(BF)
    share = jnp.where(placed, share, 0.0)
    eye = lax.broadcasted_iota(jnp.int32, (128, 128), 0) == lax.broadcasted_iota(
        jnp.int32, (128, 128), 1
    )
    pick = mm(jnp.where(eye, 1.0, 0.0).astype(BF), pick_t, NT).astype(BF)
    share_hi = share.astype(BF)
    share_lo = (share - share_hi.astype(F32)).astype(BF)
    share_hi = jnp.concatenate([share_hi] * 4, axis=1)
    share_lo = jnp.concatenate([share_lo] * 4, axis=1)

    l_wo.wait()
    x_wo.wait_recv()
    for cp in pending:
        cp.wait_recv()

    rows = ag1[...].reshape(CHIPS * 16, 1024)
    for s in range(2):
        p0 = mm(rows, wo[s, :, 0:1024], NT).reshape(CHIPS, 16, WP)
        p1 = mm(rows, wo[s, :, 1024:2048], NT).reshape(CHIPS, 16, WP)
        u = p0[:, 0:8] + p1[:, 8:16]
        us[s] = u.reshape(4, ROWS, WP).astype(BF)
    pending = []
    for df, dc in XCORE:
        q = lax.rem(f + df, 4)
        s = lax.rem(c + dc, 2)
        pending.append(send(us.at[s, q], rb.at[f * 2 + c], pdev((df, 0, dc))))
    rb[f * 2 + c] = us[c, f]
    hidden = pad32[...]
    for cp in pending:
        cp.wait_recv()
    for k in range(8):
        hidden = hidden + rb[k].astype(F32)
    hid = hidden.astype(BF).astype(F32)
    squares = jnp.sum(hid * hid, axis=1, keepdims=True)
    sq_hi = squares.astype(BF).astype(F32)
    lane2 = lax.broadcasted_iota(jnp.int32, (ROWS, WP), 1)
    normed = jnp.where(
        lane2 == W, sq_hi, jnp.where(lane2 == W + 1, squares - sq_hi, hid * pad1[...])
    ).astype(BF)
    tok[...] = mm(pick, normed).astype(BF).reshape(8, SLOT, WP)

    pending = []
    for o in PLANE:
        e = lax.rem(f + o[0], 4) * 2 + lax.rem(c + o[2], 2)
        pending.append(send(tok.at[e], xb.at[c, r * 4 + f], pdev(o)))
    xb[c, r * 4 + f] = tok[f * 2 + c]
    l_wg.wait()
    x_wg.wait_recv()
    l_wu.wait()
    x_wu.wait_recv()
    for cp in pending:
        cp.wait_recv()
    x0 = xb[0].reshape(256, WP)
    x1 = xb[1].reshape(256, WP)
    ones = lax.broadcasted_iota(jnp.int32, (16, WP), 1)
    ones = jnp.where((ones == W) | (ones == W + 1), 1.0, 0.0).astype(BF)
    sq = (mm(ones, x0, NT) + mm(ones, x1, NT))[0:1, :]
    sq_hi = sq.astype(BF).astype(F32)
    sq_lo = sq - sq_hi
    gate = mm(x0, wg[0]) + mm(x1, wg[1])
    slot = lax.rem(lax.broadcasted_iota(jnp.int32, (256, 256), 0), SLOT)
    head = jnp.where(slot == CAP, sq_hi, jnp.where(slot == CAP + 1, sq_lo, gate[:, 0:256]))
    pb[:, :, 0:256] = head.astype(BF).reshape(CHIPS, SLOT, 256)
    pb[:, :, 256:EFF] = gate[:, 256:EFF].astype(BF).reshape(CHIPS, SLOT, EFF - 256)
    up = mm(x0, wu[0]) + mm(x1, wu[1])
    pb[:, :, EFF : 2 * EFF] = up.astype(BF).reshape(CHIPS, SLOT, EFF)

    near = {}
    for k, (o, d) in enumerate(((7, -1), (5, 1))):
        for side, sgn in enumerate((1, -1)):
            near[side, k] = send(pb.at[zidx(-sgn * o)], r1.at[side, k], zdev(sgn * d))
    anti = send(pb.at[zidx(8)], ra, zdev(-2 * sg))
    for k, (o, d) in enumerate(((4, -1), (2, 1))):
        for side, sgn in enumerate((1, -1)):
            near[side, k + 2] = send(pb.at[zidx(-sgn * o)], r1.at[side, k + 2], zdev(sgn * d))
    pending = []
    for side, sgn in enumerate((1, -1)):
        near[side, 0].wait_recv()
        near[side, 1].wait_recv()
    anti.wait_recv()
    for side, sgn in enumerate((1, -1)):
        t = zidx(-sgn * 6)
        acc = pb[t].astype(F32) + r1[side, 0].astype(F32) + r1[side, 1].astype(F32)
        acc = acc + jnp.where(c == side, ra[...].astype(F32), 0.0)
        s2[side, 0] = acc.astype(BF)
        pending.append(send(s2.at[side, 0], r2.at[side, 0], zdev(-sgn * 6)))
    for side, sgn in enumerate((1, -1)):
        near[side, 2].wait_recv()
        near[side, 3].wait_recv()
        t = zidx(-sgn * 3)
        acc = pb[t].astype(F32) + r1[side, 2].astype(F32) + r1[side, 3].astype(F32)
        s2[side, 1] = acc.astype(BF)
        pending.append(send(s2.at[side, 1], r2.at[side, 1], zdev(-sgn * 3)))
    for side, sgn in enumerate((1, -1)):
        pending.append(send(pb.at[zidx(-sgn)], r2.at[side, 2], zdev(-sgn)))
    total = pb[z].astype(F32)
    for cp in pending:
        cp.wait_recv()
    for side in range(2):
        for k in range(3):
            total = total + r2[side, k].astype(F32)
    sq = total[CAP : CAP + 1, 0:256] + total[CAP + 1 : CAP + 2, 0:256]
    row = lax.broadcasted_iota(jnp.int32, (SLOT, 256), 0)
    lane3 = lax.broadcasted_iota(jnp.int32, (SLOT, 256), 1)
    sq = jnp.sum(jnp.where(lane3 == z * SLOT + row, sq, 0.0), axis=1, keepdims=True)
    rinv = lax.rsqrt(sq / D + 1e-6)
    gate = total[:, 0:EFF] * rinv
    up = total[:, EFF : 2 * EFF] * rinv
    act = gate / (1.0 + jnp.exp(-gate)) * up
    live = lax.broadcasted_iota(jnp.int32, (SLOT, EFF), 0) < CAP
    ag2[z] = jnp.where(live, act, 0.0).astype(BF)

    pending = gather_z(ag2)
    l_wd.wait()
    x_wd.wait_recv()
    for cp in pending:
        cp.wait_recv()
    rows = ag2[...].reshape(256, EFF)
    for s in range(2):
        eb[s] = mm(rows, wd[s], NT).astype(BF).reshape(16, SLOT, WP)

    pending = []
    for o in PLANE:
        b = lax.rem(r + o[1], 4) * 4 + lax.rem(f + o[0], 4)
        s = lax.rem(c + o[2], 2)
        pending.append(send(eb.at[s, b], rr.at[r * 8 + f * 2 + c], pdev(o)))
    rr[r * 8 + f * 2 + c] = eb[c, r * 4 + f]
    for cp in pending:
        cp.wait_recv()
    back = rr[...].reshape(512, WP)
    mixed = hidden + mm(share_hi, back) + mm(share_lo, back)
    out_ref[0] = mixed[:, 0:W]
    for cp in sent:
        cp.wait_send()


N_SENT = 5 + 15 + 7 + 31 + 9 + 6 + 15 + 31


def per_device(q, k, v, lens, wo, res, gain, ids, gw, wg, wu, wd):
    any_spec = pl.BlockSpec(memory_space=pl.ANY)
    vm = pltpu.VMEM
    dma = pltpu.SemaphoreType.DMA
    return pl.pallas_call(
        kernel,
        name="layer",
        out_shape=jax.ShapeDtypeStruct((1, ROWS, W), F32),
        in_specs=[any_spec] * 12,
        out_specs=pl.BlockSpec(memory_space=pltpu.VMEM),
        scratch_shapes=[
            vm((4, 4096), BF),
            vm((4, 256, HD), BF),
            vm((4, 256, HD), BF),
            vm((1, 4), jnp.int32),
            vm((ROWS, W), BF),
            vm((1, W), F32),
            vm((ROWS, 3), jnp.int32),
            vm((ROWS, 3), F32),
            vm((2, WP, KH), BF),
            vm((2, WP, EFF), BF),
            vm((2, WP, EFF), BF),
            vm((2, WP, EFF), BF),
            vm((64, HD), F32),
            vm((2, 16, 1024), F32),
            vm((16, 1024), BF),
            vm((16, 1024), BF),
            vm((CHIPS, 16, 1024), BF),
            vm((2, 4, ROWS, WP), BF),
            vm((8, ROWS, WP), BF),
            vm((ROWS, WP), F32),
            vm((1, WP), F32),
            vm((8, SLOT, WP), BF),
            vm((2, 16, SLOT, WP), BF),
            vm((CHIPS, SLOT, 2 * EFF), BF),
            vm((2, 4, SLOT, 2 * EFF), BF),
            vm((SLOT, 2 * EFF), BF),
            vm((2, 2, SLOT, 2 * EFF), BF),
            vm((2, 3, SLOT, 2 * EFF), BF),
            vm((CHIPS, SLOT, EFF), BF),
            vm((2, 16, SLOT, WP), BF),
            vm((32, SLOT, WP), BF),
            dma((12,)),
            dma((N_SENT,)),
            dma((N_SENT,)),
        ],
        compiler_params=pltpu.CompilerParams(
            collective_id=0, has_side_effects=True, vmem_limit_bytes=56 * 1024 * 1024
        ),
    )(q, k, v, lens, wo, res, gain.reshape(1, W), ids, gw, wg, wu, wd)


def solution(mesh):
    in_specs = (
        P("rep", "attn", "ffn"),
        P("rep", "attn", None, None),
        P("rep", "attn", None, None),
        P("rep", "attn"),
        P("attn", "ffn"),
        P("rep", "ffn", "attn"),
        P("attn"),
        P("rep", "ffn", None),
        P("rep", "ffn", None),
        P("ffn", "attn", "rep"),
        P("ffn", "attn", "rep"),
        P("ffn", "attn", "rep"),
    )
    out_specs = P("rep", "ffn", "attn")
    return jax.shard_map(
        per_device, mesh=mesh, in_specs=in_specs, out_specs=out_specs, check_vma=False
    )
```

time: 494 us -> 85 us (0.17)
  the two profiles are of different devices: /device:TPU:6 before, /device:TPU:1 now
where the time goes in v1:
time: 85 us; the launch traced here: 84.8 us
  Pallas kernels  80.7 us (95%)
  local copies, waits for them, and re-layouts  4.1 us (5%)
    pallas_call x1, Pallas kernels, per_device(): pl.pallas_call(kernel, name='layer', out_shape=jax.ShapeDtypeStruct((1, R...  80.7 us
    unnamed x3, local copies, waits for them, and re-layouts  4.1 us

profile of v1, /device:TPU:1, one launch (start us, length us, event | category | flops | bytes accessed | tf_op | source)
XLA Modules:
  0.0 84.8 jit_solution(12613350953708171612)
XLA Ops:
  0.0 1.4 %copy.13.ids_h = s32[1,32,3]{2,1,0:T(8,128)} copy(s32[1,32,3]{1,0,2:T(1,128)} %param.19) | data formatting | bytes 768 | tf_op args[7]
  1.4 1.4 %copy.14.gw_h = f32[1,32,3]{2,1,0:T(8,128)} copy(f32[1,32,3]{1,0,2:T(1,128)} %param.20) | data formatting | bytes 768 | tf_op args[8]
  2.7 80.7 %layer.1 = f32[1,32,224]{2,1,0:T(8,128)} custom-call(bf16[1,4,4096]{2,1,0:T(4,128)(2,1)} %q_h.1, bf16[1,4,256,256]{3,2,1,0:T(8,128)(2,1)} %k_h.1, bf16[1,4,256,256]{3,2,1,0:T(8,128)(2,1)} %v_h.1, s32[1,4]{1,0:T(1,128)} %len_h.1, bf16[224,4096]{1,0:T(8,128)(2,1)} %wo_h.1, bf16[1,32,224]{2,1,0:T(8,128)(2,1)} %res_h.1, f32[1,224]{1,0:T(1,128)} %bitcast.1, ...), custom_call_target="tpu_custom_call" | custom-call | tf_op jit(solution)/shard_map/layer/pallas_call | solution.py:336
  83.4 1.4 %copy.16 = f32[1,32,224]{2,1,0:T(8,128)} copy(f32[1,32,224]{2,1,0:T(8,128)} %layer.1) | data formatting | bytes 57344

commit v2 on v1

--- a/solution.py
+++ b/solution.py
@@ -34,6 +34,8 @@
     key=lambda o: (-min(o[0], 4 - o[0]), o),
 )
 
+RELAY = {0: (5, 1), 1: (4, 3, 2), 5: (8, 7, 6)}
+
 
 def mm(a, b, dims=NN):
     return lax.dot_general(a, b, dims, preferred_element_type=F32)
@@ -44,7 +46,7 @@
     out_ref,
     qv, kv, vv, lenv, resv, gainv, idsv, gwv, wo, wg, wu, wd,
     qs, att, xs, xr, ag1, us, rb, pad32, pad1, tok, xb, pb, r1, ra, s2, r2, ag2, eb, rr,
-    ld, ss, rs,
+    ld, ss, rs, stay_s, back_s,
 ):
     a = lax.axis_index("attn")
     f = lax.axis_index("ffn")
@@ -79,10 +81,11 @@
 
     sent = []
 
-    def send(src, dst, dev):
+    def send(src, dst, dev, arrival=None):
         k = len(sent)
         cp = pltpu.make_async_remote_copy(
-            src_ref=src, dst_ref=dst, send_sem=ss.at[k], recv_sem=rs.at[k],
+            src_ref=src, dst_ref=dst, send_sem=ss.at[k],
+            recv_sem=rs.at[k] if arrival is None else arrival,
             device_id=dev, device_id_type=MESH,
         )
         cp.start()
@@ -93,16 +96,17 @@
     l_k = load(k_h.at[0], kv)
     l_v = load(v_h.at[0], vv)
     l_len = load(len_h, lenv)
-    l_ids = load(ids_h.at[0], idsv)
-    l_gw = load(gw_h.at[0], gwv)
+
+    barrier = pltpu.get_barrier_semaphore()
+    peers = [zdev(d) for d in (5, -5)] + [pdev(o) for o in PLANE]
+    peers += [zdev(d) for d in (3, -3, 2, -2, 1, -1)]
+    for dev in peers:
+        pl.semaphore_signal(barrier, inc=1, device_id=dev, device_id_type=MESH)
+
+    l_ids = load(ids_h, idsv)
+    l_gw = load(gw_h, gwv)
     l_res = load(res_h.at[0], resv)
     l_gain = load(gain_h, gainv)
-
-    barrier = pltpu.get_barrier_semaphore()
-    peers = [pdev(o) for o in PLANE] + [zdev(d) for d in (6, -6, 3, -3, 2, -2, 1, -1)]
-    for dev in peers:
-        pl.semaphore_signal(barrier, inc=1, device_id=dev, device_id_type=MESH)
-
     half = pl.multiple_of(c * KH, KH)
     other = pl.multiple_of((1 - c) * KH, KH)
     l_wo = load(wo_h.at[:, pl.ds(half, KH)], wo.at[c, pl.ds(0, W)])
@@ -141,29 +145,47 @@
     x_wu = send(wu_h.at[1 - c], wu.at[c, pl.ds(0, W)], sib)
     x_wd = send(wd_h.at[1 - c], wd.at[c, pl.ds(0, W)], sib)
 
-    def gather_z(buf):
-        own = buf.at[z]
-        first = {d: send(own, own, zdev(d)) for d in (6, -6, 3, -3, 1, -1)}
-        rest = []
-        first[6].wait_recv()
-        far = buf.at[zidx(-6)]
-        rest += [send(far, far, zdev(1)), send(far, far, zdev(-1))]
-        first[-6].wait_recv()
-        far = buf.at[zidx(6)]
-        rest += [send(far, far, zdev(-1)), send(far, far, zdev(1))]
-        far = buf.at[zidx(-6 * sg)]
-        rest += [send(far, far, zdev(2 * sg))]
-        first[3].wait_recv()
-        far = buf.at[zidx(-3)]
-        rest += [send(far, far, zdev(1)), send(far, far, zdev(-1))]
-        first[-3].wait_recv()
-        far = buf.at[zidx(3)]
-        rest += [send(far, far, zdev(-1)), send(far, far, zdev(1))]
-        return [first[1], first[-1]] + rest
+    def gather_z(buf, arrived=None):
+        got = {}
+
+        def pass_on(o):
+            block = buf.at[zidx(-o)]
+            for to in RELAY[abs(o)]:
+                if o == 0:
+                    got[to] = send(block, block, zdev(to))
+                    got[-to] = send(block, block, zdev(-to))
+                elif to < 8:
+                    sgn = 1 if o > 0 else -1
+                    got[sgn * to] = send(block, block, zdev(sgn * to - o))
+
+        pass_on(0)
+        yield
+        for o in (1, 5):
+            for sgn in (1, -1):
+                got[sgn * o].wait_recv()
+                if o == 5 and sgn == -1:
+                    far = buf.at[zidx(-5 * sg)]
+                    got[8] = send(far, far, zdev(3 * sg))
+                    pass_on(5)
+                if o == 1 or sgn == -1:
+                    pass_on(sgn * o)
+            if o == 1 and arrived is not None:
+                arrived((0, 1, -1))
+        rest = [2, -2, 3, -3, 4, -4]
+        for o in rest:
+            got[o].wait_recv()
+        if arrived is not None:
+            arrived([5, -5] + rest)
+        last = [6, -6, 7, -7, 8]
+        for o in last:
+            got[o].wait_recv()
+        if arrived is not None:
+            arrived(last)
 
     x_cp.wait_recv()
     ag1[z] = jnp.where(mine, att[c], 0.0).astype(BF) + xr[...]
-    pending = gather_z(ag1)
+    heads = gather_z(ag1)
+    next(heads)
 
     for buf in (wo, wg, wu, wd):
         buf[:, W:WP, :] = jnp.zeros((2, WP - W, buf.shape[2]), BF)
@@ -175,35 +197,34 @@
     pad32[:, 0:W] = resv[...].astype(F32)
     pad1[...] = jnp.zeros((1, WP), F32)
     pad1[:, 0:W] = gainv[...]
-    lane = lax.broadcasted_iota(jnp.int32, (ROWS, 128), 1)
-    ids = idsv[...]
-    gws = gwv[...]
-    hits = jnp.zeros((ROWS, 128), F32)
-    share = jnp.zeros((ROWS, 128), F32)
+    spot = lax.broadcasted_iota(jnp.int32, (128, ROWS), 0)
+    hits = jnp.zeros((128, ROWS), F32)
+    share = jnp.zeros((128, ROWS), F32)
     for k in range(3):
-        same = ids[:, k : k + 1] == lax.div(lane, SLOT)
+        same = idsv[k] == lax.div(spot, SLOT)
         hits = hits + jnp.where(same, 1.0, 0.0)
-        share = share + jnp.where(same, gws[:, k : k + 1], 0.0)
-    lower = lax.broadcasted_iota(jnp.int32, (ROWS, ROWS), 0) > lax.broadcasted_iota(
+        share = share + jnp.where(same, gwv[k], 0.0)
+    earlier = lax.broadcasted_iota(jnp.int32, (ROWS, ROWS), 0) < lax.broadcasted_iota(
         jnp.int32, (ROWS, ROWS), 1
     )
-    before = mm(jnp.where(lower, 1.0, 0.0).astype(BF), hits.astype(BF))
-    placed = before == lax.rem(lane, SLOT).astype(F32)
-    pick_t = jnp.where(placed, hits, 0.0).astype(BF)
+    before = mm(hits.astype(BF), jnp.where(earlier, 1.0, 0.0).astype(BF))
+    placed = before == lax.rem(spot, SLOT).astype(F32)
+    pick = jnp.where(placed, hits, 0.0).astype(BF)
     share = jnp.where(placed, share, 0.0)
-    eye = lax.broadcasted_iota(jnp.int32, (128, 128), 0) == lax.broadcasted_iota(
-        jnp.int32, (128, 128), 1
+    eye = lax.broadcasted_iota(jnp.int32, (ROWS, ROWS), 0) == lax.broadcasted_iota(
+        jnp.int32, (ROWS, ROWS), 1
     )
-    pick = mm(jnp.where(eye, 1.0, 0.0).astype(BF), pick_t, NT).astype(BF)
+    eye = jnp.where(eye, 1.0, 0.0).astype(BF)
     share_hi = share.astype(BF)
     share_lo = (share - share_hi.astype(F32)).astype(BF)
-    share_hi = jnp.concatenate([share_hi] * 4, axis=1)
-    share_lo = jnp.concatenate([share_lo] * 4, axis=1)
-
+    share_hi = jnp.concatenate([mm(eye, share_hi, NT).astype(BF)] * 4, axis=1)
+    share_lo = jnp.concatenate([mm(eye, share_lo, NT).astype(BF)] * 4, axis=1)
+
+
+    for _ in heads:
+        pass
     l_wo.wait()
     x_wo.wait_recv()
-    for cp in pending:
-        cp.wait_recv()
 
     rows = ag1[...].reshape(CHIPS * 16, 1024)
     for s in range(2):
@@ -257,34 +278,37 @@
     up = mm(x0, wu[0]) + mm(x1, wu[1])
     pb[:, :, EFF : 2 * EFF] = up.astype(BF).reshape(CHIPS, SLOT, EFF)
 
-    near = {}
-    for k, (o, d) in enumerate(((7, -1), (5, 1))):
-        for side, sgn in enumerate((1, -1)):
-            near[side, k] = send(pb.at[zidx(-sgn * o)], r1.at[side, k], zdev(sgn * d))
-    anti = send(pb.at[zidx(8)], ra, zdev(-2 * sg))
-    for k, (o, d) in enumerate(((4, -1), (2, 1))):
-        for side, sgn in enumerate((1, -1)):
-            near[side, k + 2] = send(pb.at[zidx(-sgn * o)], r1.at[side, k + 2], zdev(sgn * d))
+    sides = ((0, 1), (1, -1))
+    leaf = {}
+    for side, sgn in sides:
+        leaf[side, 7] = send(pb.at[zidx(-sgn * 7)], r1.at[side, 0], zdev(-sgn))
+    anti = send(pb.at[zidx(8)], ra, zdev(-3 * sg))
+    for k, o in ((2, 4), (3, 2)):
+        for side, sgn in sides:
+            leaf[side, o] = send(pb.at[zidx(-sgn * o)], r1.at[side, k], zdev(-sgn))
     pending = []
-    for side, sgn in enumerate((1, -1)):
-        near[side, 0].wait_recv()
-        near[side, 1].wait_recv()
-    anti.wait_recv()
-    for side, sgn in enumerate((1, -1)):
-        t = zidx(-sgn * 6)
-        acc = pb[t].astype(F32) + r1[side, 0].astype(F32) + r1[side, 1].astype(F32)
-        acc = acc + jnp.where(c == side, ra[...].astype(F32), 0.0)
+    for side, sgn in sides:
+        leaf[side, 7].wait_recv()
+        acc = pb[zidx(-sgn * 6)].astype(F32) + r1[side, 0].astype(F32)
         s2[side, 0] = acc.astype(BF)
-        pending.append(send(s2.at[side, 0], r2.at[side, 0], zdev(-sgn * 6)))
-    for side, sgn in enumerate((1, -1)):
-        near[side, 2].wait_recv()
-        near[side, 3].wait_recv()
-        t = zidx(-sgn * 3)
-        acc = pb[t].astype(F32) + r1[side, 2].astype(F32) + r1[side, 3].astype(F32)
+        leaf[side, 6] = send(s2.at[side, 0], r1.at[side, 1], zdev(-sgn))
+    for side, sgn in sides:
+        leaf[side, 4].wait_recv()
+        acc = pb[zidx(-sgn * 3)].astype(F32) + r1[side, 2].astype(F32)
         s2[side, 1] = acc.astype(BF)
         pending.append(send(s2.at[side, 1], r2.at[side, 1], zdev(-sgn * 3)))
-    for side, sgn in enumerate((1, -1)):
-        pending.append(send(pb.at[zidx(-sgn)], r2.at[side, 2], zdev(-sgn)))
+    anti.wait_recv()
+    for side, sgn in sides:
+        leaf[side, 6].wait_recv()
+        acc = pb[zidx(-sgn * 5)].astype(F32) + r1[side, 1].astype(F32)
+        acc = acc + jnp.where(c == side, ra[...].astype(F32), 0.0)
+        s2[side, 2] = acc.astype(BF)
+        pending.append(send(s2.at[side, 2], r2.at[side, 0], zdev(-sgn * 5)))
+    for side, sgn in sides:
+        leaf[side, 2].wait_recv()
+        acc = pb[zidx(-sgn)].astype(F32) + r1[side, 3].astype(F32)
+        s2[side, 3] = acc.astype(BF)
+        pending.append(send(s2.at[side, 3], r2.at[side, 2], zdev(-sgn)))
     total = pb[z].astype(F32)
     for cp in pending:
         cp.wait_recv()
@@ -302,41 +326,69 @@
     live = lax.broadcasted_iota(jnp.int32, (SLOT, EFF), 0) < CAP
     ag2[z] = jnp.where(live, act, 0.0).astype(BF)
 
-    pending = gather_z(ag2)
     l_wd.wait()
     x_wd.wait_recv()
-    for cp in pending:
-        cp.wait_recv()
-    rows = ag2[...].reshape(256, EFF)
-    for s in range(2):
-        eb[s] = mm(rows, wd[s], NT).astype(BF).reshape(16, SLOT, WP)
-
-    pending = []
-    for o in PLANE:
-        b = lax.rem(r + o[1], 4) * 4 + lax.rem(f + o[0], 4)
-        s = lax.rem(c + o[2], 2)
-        pending.append(send(eb.at[s, b], rr.at[r * 8 + f * 2 + c], pdev(o)))
-    rr[r * 8 + f * 2 + c] = eb[c, r * 4 + f]
-    for cp in pending:
-        cp.wait_recv()
+    me = r * 8 + f * 2 + c
+    stay = []
+
+    def give_back(offsets):
+        first = len(stay)
+        rows = jnp.concatenate([ag2[zidx(-o)] for o in offsets], axis=0)
+        for s in range(2):
+            out = mm(rows, wd[s], NT).astype(BF).reshape(len(offsets), SLOT, WP)
+            eb[s, first : first + len(offsets)] = out
+        for k, o in enumerate(offsets):
+            b = zidx(-o)
+            fo, ro = lax.rem(b, 4), lax.div(b, 4)
+            i = first + k
+            send(eb.at[1 - c, i], rr.at[me], {"attn": z * 2 + 1 - c, "ffn": fo, "rep": ro}, back_s.at[me])
+            cp = pltpu.make_async_remote_copy(
+                src_ref=eb.at[c, i], dst_ref=rr.at[me], send_sem=stay_s.at[i],
+                recv_sem=back_s.at[me], device_id={"ffn": fo, "rep": ro}, device_id_type=MESH,
+            )
+            away = b != r * 4 + f
+            stay.append((away, cp))
+
+            @pl.when(away)
+            def _():
+                cp.start()
+
+            @pl.when(jnp.logical_not(away))
+            def _():
+                rr[me] = eb[c, i]
+
+    for _ in gather_z(ag2, give_back):
+        pass
+    for j in range(1, 32):
+        k = lax.rem(me + j, 32)
+        pltpu.make_async_remote_copy(
+            src_ref=eb.at[0, 0], dst_ref=rr.at[k], send_sem=stay_s.at[0],
+            recv_sem=back_s.at[k], device_id=sib, device_id_type=MESH,
+        ).wait_recv()
     back = rr[...].reshape(512, WP)
     mixed = hidden + mm(share_hi, back) + mm(share_lo, back)
     out_ref[0] = mixed[:, 0:W]
     for cp in sent:
         cp.wait_send()
-
-
-N_SENT = 5 + 15 + 7 + 31 + 9 + 6 + 15 + 31
+    for away, cp in stay:
+        @pl.when(away)
+        def _():
+            cp.wait_send()
+
+
+N_SENT = 5 + 15 + 7 + 31 + 15 + 15 + 16
 
 
 def per_device(q, k, v, lens, wo, res, gain, ids, gw, wg, wu, wd):
+    ids = jnp.transpose(ids, (2, 0, 1))
+    gw = jnp.transpose(gw, (2, 0, 1))
     any_spec = pl.BlockSpec(memory_space=pl.ANY)
     vm = pltpu.VMEM
     dma = pltpu.SemaphoreType.DMA
     return pl.pallas_call(
         kernel,
         name="layer",
-        out_shape=jax.ShapeDtypeStruct((1, ROWS, W), F32),
+        out_shape=pltpu.VMEM((1, ROWS, W), F32),
         in_specs=[any_spec] * 12,
         out_specs=pl.BlockSpec(memory_space=pltpu.VMEM),
         scratch_shapes=[
@@ -346,8 +398,8 @@
             vm((1, 4), jnp.int32),
             vm((ROWS, W), BF),
             vm((1, W), F32),
-            vm((ROWS, 3), jnp.int32),
-            vm((ROWS, 3), F32),
+            vm((3, 1, ROWS), jnp.int32),
+            vm((3, 1, ROWS), F32),
             vm((2, WP, KH), BF),
             vm((2, WP, EFF), BF),
             vm((2, WP, EFF), BF),
@@ -366,7 +418,7 @@
             vm((CHIPS, SLOT, 2 * EFF), BF),
             vm((2, 4, SLOT, 2 * EFF), BF),
             vm((SLOT, 2 * EFF), BF),
-            vm((2, 2, SLOT, 2 * EFF), BF),
+            vm((2, 4, SLOT, 2 * EFF), BF),
             vm((2, 3, SLOT, 2 * EFF), BF),
             vm((CHIPS, SLOT, EFF), BF),
             vm((2, 16, SLOT, WP), BF),
@@ -374,6 +426,8 @@
             dma((12,)),
             dma((N_SENT,)),
             dma((N_SENT,)),
+            dma((16,)),
+            dma((32,)),
         ],
         compiler_params=pltpu.CompilerParams(
             collective_id=0, has_side_effects=True, vmem_limit_bytes=56 * 1024 * 1024

time: 85 us -> 78.4 us (0.922)
  the two profiles are of different devices: /device:TPU:1 before, /device:TPU:16 now
where the time goes in v2:
time: 78.4 us; the launch traced here: 78.3 us
  Pallas kernels  77.6 us (99%)
    pallas_call x1, Pallas kernels, per_device(): pl.pallas_call(kernel, name='layer', out_shape=pltpu.VMEM((1, ROWS, W), F...  77.6 us

profile of v2, /device:TPU:16, one launch (start us, length us, event | category | flops | bytes accessed | tf_op | source)
XLA Modules:
  0.0 78.3 jit_solution(14531665138405550980)
XLA Ops:
  0.0 77.6 %layer.1 = f32[1,32,224]{2,1,0:T(8,128)S(1)} custom-call(bf16[1,4,4096]{2,1,0:T(4,128)(2,1)} %q_h.1, bf16[1,4,256,256]{3,2,1,0:T(8,128)(2,1)} %k_h.1, bf16[1,4,256,256]{3,2,1,0:T(8,128)(2,1)} %v_h.1, s32[1,4]{1,0:T(1,128)} %len_h.1, bf16[224,4096]{1,0:T(8,128)(2,1)} %wo_h.1, bf16[1,32,224]{2,1,0:T(8,128)(2,1)} %res_h.1, f32[1,224]{1,0:T(1,128)} %bitcast.5, ...), custom_call_target="tpu_custom_call" | custom-call | tf_op jit(solution)/shard_map/layer/pallas_call | solution.py:388
  77.6 0.6 copy.14

commit v3 on v2

--- a/solution.py
+++ b/solution.py
@@ -21,6 +21,8 @@
 SLOT = 16
 ROWS = 32
 EFF = 640
+EA, EB = 384, 256
+TAIL = 512
 HD = 256
 KH = 2048
 D = 7168
@@ -34,6 +36,9 @@
     key=lambda o: (-min(o[0], 4 - o[0]), o),
 )
 
+FIRST = (0, 1, -1)
+MIDDLE = (5, -5, 2, -2, 3, -3, 4, -4)
+LAST = (6, -6, 7, -7, 8)
 RELAY = {0: (5, 1), 1: (4, 3, 2), 5: (8, 7, 6)}
 
 
@@ -45,7 +50,7 @@
     q_h, k_h, v_h, len_h, wo_h, res_h, gain_h, ids_h, gw_h, wg_h, wu_h, wd_h,
     out_ref,
     qv, kv, vv, lenv, resv, gainv, idsv, gwv, wo, wg, wu, wd,
-    qs, att, xs, xr, ag1, us, rb, pad32, pad1, tok, xb, pb, r1, ra, s2, r2, ag2, eb, rr,
+    qs, att, xs, xr, ag1, us, rb, pad32, pad1, tok, xb, pb_a, r1_a, ra_a, s2_a, r2_a, pb_b, r1_b, ra_b, s2_b, r2_b, last_up, ag2_a, ag2_b, eb, rr,
     ld, ss, rs, stay_s, back_s,
 ):
     a = lax.axis_index("attn")
@@ -145,7 +150,7 @@
     x_wu = send(wu_h.at[1 - c], wu.at[c, pl.ds(0, W)], sib)
     x_wd = send(wd_h.at[1 - c], wd.at[c, pl.ds(0, W)], sib)
 
-    def gather_z(buf, arrived=None):
+    def gather_z(buf):
         got = {}
 
         def pass_on(o):
@@ -160,27 +165,22 @@
 
         pass_on(0)
         yield
-        for o in (1, 5):
-            for sgn in (1, -1):
-                got[sgn * o].wait_recv()
-                if o == 5 and sgn == -1:
-                    far = buf.at[zidx(-5 * sg)]
-                    got[8] = send(far, far, zdev(3 * sg))
-                    pass_on(5)
-                if o == 1 or sgn == -1:
-                    pass_on(sgn * o)
-            if o == 1 and arrived is not None:
-                arrived((0, 1, -1))
-        rest = [2, -2, 3, -3, 4, -4]
-        for o in rest:
+        for sgn in (1, -1):
+            got[sgn].wait_recv()
+            pass_on(sgn)
+        yield
+        got[5].wait_recv()
+        got[-5].wait_recv()
+        far = buf.at[zidx(-5 * sg)]
+        got[8] = send(far, far, zdev(3 * sg))
+        pass_on(5)
+        pass_on(-5)
+        yield
+        for o in MIDDLE[2:]:
             got[o].wait_recv()
-        if arrived is not None:
-            arrived([5, -5] + rest)
-        last = [6, -6, 7, -7, 8]
-        for o in last:
+        yield
+        for o in LAST:
             got[o].wait_recv()
-        if arrived is not None:
-            arrived(last)
 
     x_cp.wait_recv()
     ag1[z] = jnp.where(mine, att[c], 0.0).astype(BF) + xr[...]
@@ -270,61 +270,105 @@
     sq = (mm(ones, x0, NT) + mm(ones, x1, NT))[0:1, :]
     sq_hi = sq.astype(BF).astype(F32)
     sq_lo = sq - sq_hi
-    gate = mm(x0, wg[0]) + mm(x1, wg[1])
-    slot = lax.rem(lax.broadcasted_iota(jnp.int32, (256, 256), 0), SLOT)
-    head = jnp.where(slot == CAP, sq_hi, jnp.where(slot == CAP + 1, sq_lo, gate[:, 0:256]))
-    pb[:, :, 0:256] = head.astype(BF).reshape(CHIPS, SLOT, 256)
-    pb[:, :, 256:EFF] = gate[:, 256:EFF].astype(BF).reshape(CHIPS, SLOT, EFF - 256)
-    up = mm(x0, wu[0]) + mm(x1, wu[1])
-    pb[:, :, EFF : 2 * EFF] = up.astype(BF).reshape(CHIPS, SLOT, EFF)
+    def project(w, lo, hi):
+        out = mm(x0, w[0, :, lo:hi]) + mm(x1, w[1, :, lo:hi])
+        return out.reshape(CHIPS, SLOT, hi - lo)
+
+    tail = project(wu, TAIL, EFF)
+    slot = lax.broadcasted_iota(jnp.int32, (CHIPS, SLOT, 128), 1)
+
+    def put(buf, column, base, first_tile):
+        for j in range(base.shape[2] // 128):
+            t = first_tile + j
+            if t in (2, 3):
+                low = sq_hi[:, (t - 2) * 128 : (t - 1) * 128].reshape(1, 1, 128)
+            elif t in (4, 5):
+                low = sq_lo[:, (t - 4) * 128 : (t - 3) * 128].reshape(1, 1, 128)
+            else:
+                k = 9 + t if t < 2 else 5 + t
+                low = tail[:, k : k + 1, :]
+            piece = jnp.where(slot == CAP + 1, low, base[:, :, j * 128 : (j + 1) * 128])
+            piece = jnp.where(slot == CAP, tail[:, t : t + 1, :], piece)
+            buf[:, :, column + j * 128 : column + (j + 1) * 128] = piece.astype(BF)
 
     sides = ((0, 1), (1, -1))
-    leaf = {}
-    for side, sgn in sides:
-        leaf[side, 7] = send(pb.at[zidx(-sgn * 7)], r1.at[side, 0], zdev(-sgn))
-    anti = send(pb.at[zidx(8)], ra, zdev(-3 * sg))
-    for k, o in ((2, 4), (3, 2)):
-        for side, sgn in sides:
-            leaf[side, o] = send(pb.at[zidx(-sgn * o)], r1.at[side, k], zdev(-sgn))
-    pending = []
-    for side, sgn in sides:
-        leaf[side, 7].wait_recv()
-        acc = pb[zidx(-sgn * 6)].astype(F32) + r1[side, 0].astype(F32)
-        s2[side, 0] = acc.astype(BF)
-        leaf[side, 6] = send(s2.at[side, 0], r1.at[side, 1], zdev(-sgn))
-    for side, sgn in sides:
-        leaf[side, 4].wait_recv()
-        acc = pb[zidx(-sgn * 3)].astype(F32) + r1[side, 2].astype(F32)
-        s2[side, 1] = acc.astype(BF)
-        pending.append(send(s2.at[side, 1], r2.at[side, 1], zdev(-sgn * 3)))
-    anti.wait_recv()
-    for side, sgn in sides:
-        leaf[side, 6].wait_recv()
-        acc = pb[zidx(-sgn * 5)].astype(F32) + r1[side, 1].astype(F32)
-        acc = acc + jnp.where(c == side, ra[...].astype(F32), 0.0)
-        s2[side, 2] = acc.astype(BF)
-        pending.append(send(s2.at[side, 2], r2.at[side, 0], zdev(-sgn * 5)))
-    for side, sgn in sides:
-        leaf[side, 2].wait_recv()
-        acc = pb[zidx(-sgn)].astype(F32) + r1[side, 3].astype(F32)
-        s2[side, 3] = acc.astype(BF)
-        pending.append(send(s2.at[side, 3], r2.at[side, 2], zdev(-sgn)))
-    total = pb[z].astype(F32)
-    for cp in pending:
-        cp.wait_recv()
-    for side in range(2):
-        for k in range(3):
-            total = total + r2[side, k].astype(F32)
-    sq = total[CAP : CAP + 1, 0:256] + total[CAP + 1 : CAP + 2, 0:256]
+
+    class Sum:
+        def __init__(self, pb, r1, ra, s2, r2):
+            self.pb, self.r1, self.ra, self.s2, self.r2 = pb, r1, ra, s2, r2
+            self.leaf, self.ends = {}, []
+
+        def leaves(self):
+            for k, (o, d) in enumerate(((7, -1), (5, 1), (4, -2), (3, -1), (1, 1))):
+                for side, sgn in sides:
+                    src = self.pb.at[zidx(-sgn * o)]
+                    self.leaf[side, k] = send(src, self.r1.at[side, k], zdev(sgn * d))
+                if o == 5:
+                    self.anti = send(self.pb.at[zidx(8)], self.ra, zdev(-2 * sg))
+
+        def relay(self, slot, o, parts):
+            for side, sgn in sides:
+                acc = self.pb[zidx(-sgn * o)].astype(F32)
+                for k in parts:
+                    self.leaf[side, k].wait_recv()
+                    acc = acc + self.r1[side, k].astype(F32)
+                if o == 6:
+                    if side == 0:
+                        self.anti.wait_recv()
+                    acc = acc + jnp.where(c == side, self.ra[...].astype(F32), 0.0)
+                self.s2[side, slot] = acc.astype(BF)
+                src = self.s2.at[side, slot]
+                self.ends.append(send(src, self.r2.at[side, slot], zdev(-sgn * o)))
+
+        def total(self):
+            out = self.pb[z].astype(F32)
+            for cp in self.ends:
+                cp.wait_recv()
+            for side in range(2):
+                for k in range(2):
+                    out = out + self.r2[side, k].astype(F32)
+            return out
+
+    sum_a, sum_b = Sum(pb_a, r1_a, ra_a, s2_a, r2_a), Sum(pb_b, r1_b, ra_b, s2_b, r2_b)
+    put(pb_a, 0, project(wg, 0, EA), 0)
+    put(pb_a, EA, project(wu, 0, EA), 3)
+    sum_a.leaves()
+    put(pb_b, 0, project(wg, EA, EFF), 6)
+    put(pb_b, EB, project(wu, EA, TAIL), 8)
+    sum_b.leaves()
+    sum_a.relay(0, 6, (0, 1))
+    sum_b.relay(0, 6, (0, 1))
+    sum_a.relay(1, 2, (2, 3, 4))
+    sum_b.relay(1, 2, (2, 3, 4))
+
+    def activate(gate, up):
+        gate, up = gate * rinv, up * rinv
+        act = gate / (1.0 + jnp.exp(-gate)) * up
+        live = lax.broadcasted_iota(jnp.int32, act.shape, 0) < CAP
+        return jnp.where(live, act, 0.0).astype(BF)
+
+    total = sum_a.total()
+    for t in range(6):
+        last_up[t : t + 1, :] = total[CAP : CAP + 1, t * 128 : (t + 1) * 128]
+    for t in range(2):
+        last_up[9 + t : 10 + t, :] = total[CAP + 1 : CAP + 2, t * 128 : (t + 1) * 128]
+    sq = total[CAP + 1 : CAP + 2, 256:512] + total[CAP + 1 : CAP + 2, 512:768]
     row = lax.broadcasted_iota(jnp.int32, (SLOT, 256), 0)
     lane3 = lax.broadcasted_iota(jnp.int32, (SLOT, 256), 1)
     sq = jnp.sum(jnp.where(lane3 == z * SLOT + row, sq, 0.0), axis=1, keepdims=True)
     rinv = lax.rsqrt(sq / D + 1e-6)
-    gate = total[:, 0:EFF] * rinv
-    up = total[:, EFF : 2 * EFF] * rinv
-    act = gate / (1.0 + jnp.exp(-gate)) * up
-    live = lax.broadcasted_iota(jnp.int32, (SLOT, EFF), 0) < CAP
-    ag2[z] = jnp.where(live, act, 0.0).astype(BF)
+    ag2_a[z] = activate(total[:, 0:EA], total[:, EA : 2 * EA])
+    rows_a = gather_z(ag2_a)
+    next(rows_a)
+    total = sum_b.total()
+    for t in range(3):
+        last_up[6 + t : 7 + t, :] = total[CAP : CAP + 1, t * 128 : (t + 1) * 128]
+        last_up[11 + t : 12 + t, :] = total[CAP + 1 : CAP + 2, t * 128 : (t + 1) * 128]
+    last_up[CAP:SLOT, :] = jnp.zeros((SLOT - CAP, 128), F32)
+    up = jnp.concatenate([total[:, EB : EB + 128], last_up[...]], axis=1)
+    ag2_b[z] = activate(total[:, 0:EB], up)
+    rows_b = gather_z(ag2_b)
+    next(rows_b)
 
     l_wd.wait()
     x_wd.wait_recv()
@@ -333,10 +377,11 @@
 
     def give_back(offsets):
         first = len(stay)
-        rows = jnp.concatenate([ag2[zidx(-o)] for o in offsets], axis=0)
+        act_a = jnp.concatenate([ag2_a[zidx(-o)] for o in offsets], axis=0)
+        act_b = jnp.concatenate([ag2_b[zidx(-o)] for o in offsets], axis=0)
         for s in range(2):
-            out = mm(rows, wd[s], NT).astype(BF).reshape(len(offsets), SLOT, WP)
-            eb[s, first : first + len(offsets)] = out
+            out = mm(act_a, wd[s, :, 0:EA], NT) + mm(act_b, wd[s, :, EA:EFF], NT)
+            eb[s, first : first + len(offsets)] = out.astype(BF).reshape(len(offsets), SLOT, WP)
         for k, o in enumerate(offsets):
             b = zidx(-o)
             fo, ro = lax.rem(b, 4), lax.div(b, 4)
@@ -357,8 +402,18 @@
             def _():
                 rr[me] = eb[c, i]
 
-    for _ in gather_z(ag2, give_back):
-        pass
+    next(rows_a)
+    next(rows_b)
+    next(rows_a)
+    give_back(FIRST)
+    next(rows_b)
+    next(rows_a)
+    next(rows_b)
+    give_back(MIDDLE)
+    for rows in (rows_a, rows_b):
+        for _ in rows:
+            pass
+    give_back(LAST)
     for j in range(1, 32):
         k = lax.rem(me + j, 32)
         pltpu.make_async_remote_copy(
@@ -376,7 +431,7 @@
             cp.wait_send()
 
 
-N_SENT = 5 + 15 + 7 + 31 + 15 + 15 + 16
+N_SENT = 5 + 15 + 7 + 31 + 30 + 30 + 16
 
 
 def per_device(q, k, v, lens, wo, res, gain, ids, gw, wg, wu, wd):
@@ -415,12 +470,19 @@
             vm((1, WP), F32),
             vm((8, SLOT, WP), BF),
             vm((2, 16, SLOT, WP), BF),
-            vm((CHIPS, SLOT, 2 * EFF), BF),
-            vm((2, 4, SLOT, 2 * EFF), BF),
-            vm((SLOT, 2 * EFF), BF),
-            vm((2, 4, SLOT, 2 * EFF), BF),
-            vm((2, 3, SLOT, 2 * EFF), BF),
-            vm((CHIPS, SLOT, EFF), BF),
+            vm((CHIPS, SLOT, 2 * EA), BF),
+            vm((2, 5, SLOT, 2 * EA), BF),
+            vm((SLOT, 2 * EA), BF),
+            vm((2, 2, SLOT, 2 * EA), BF),
+            vm((2, 2, SLOT, 2 * EA), BF),
+            vm((CHIPS, SLOT, EB + 128), BF),
+            vm((2, 5, SLOT, EB + 128), BF),
+            vm((SLOT, EB + 128), BF),
+            vm((2, 2, SLOT, EB + 128), BF),
+            vm((2, 2, SLOT, EB + 128), BF),
+            vm((SLOT, 128), F32),
+            vm((CHIPS, SLOT, EA), BF),
+            vm((CHIPS, SLOT, EB), BF),
             vm((2, 16, SLOT, WP), BF),
             vm((32, SLOT, WP), BF),
             dma((12,)),

time: 78.4 us -> 77.1 us (0.983)
  Pallas kernels: 77.6 us -> 76.3 us
    pallas_call x1, Pallas kernels: 77.6 us -> 76.3 us  [per_device(): pl.pallas_call(kernel, name='layer', out_shape=pltpu.VMEM((1, ROWS, W), F...]
where the time goes in v3:
time: 77.1 us; the launch traced here: 76.9 us
  Pallas kernels  76.3 us (99%)
    pallas_call x1, Pallas kernels, per_device(): pl.pallas_call(kernel, name='layer', out_shape=pltpu.VMEM((1, ROWS, W), F...  76.3 us

profile of v3, /device:TPU:16, one launch (start us, length us, event | category | flops | bytes accessed | tf_op | source)
XLA Modules:
  0.0 76.9 jit_solution(13422649018542102774)
XLA Ops:
  0.0 76.3 %layer.1 = f32[1,32,224]{2,1,0:T(8,128)S(1)} custom-call(bf16[1,4,4096]{2,1,0:T(4,128)(2,1)} %q_h.1, bf16[1,4,256,256]{3,2,1,0:T(8,128)(2,1)} %k_h.1, bf16[1,4,256,256]{3,2,1,0:T(8,128)(2,1)} %v_h.1, s32[1,4]{1,0:T(1,128)} %len_h.1, bf16[224,4096]{1,0:T(8,128)(2,1)} %wo_h.1, bf16[1,32,224]{2,1,0:T(8,128)(2,1)} %res_h.1, f32[1,224]{1,0:T(1,128)} %bitcast.5, ...), custom_call_target="tpu_custom_call" | custom-call | tf_op jit(solution)/shard_map/layer/pallas_call | solution.py:443
  76.3 0.6 copy.14

commit v4 on v3

--- a/solution.py
+++ b/solution.py
@@ -50,8 +50,8 @@
     q_h, k_h, v_h, len_h, wo_h, res_h, gain_h, ids_h, gw_h, wg_h, wu_h, wd_h,
     out_ref,
     qv, kv, vv, lenv, resv, gainv, idsv, gwv, wo, wg, wu, wd,
-    qs, att, xs, xr, ag1, us, rb, pad32, pad1, tok, xb, pb_a, r1_a, ra_a, s2_a, r2_a, pb_b, r1_b, ra_b, s2_b, r2_b, last_up, ag2_a, ag2_b, eb, rr,
-    ld, ss, rs, stay_s, back_s,
+    qs, att, xs, xr, ag1, us, rb, pad32, pad1, tok, xb, pb_a, r1_a, s2_a, r2_a, pb_b, r1_b, s2_b, r2_b, last_up, ag2_a, ag2_b, eb, rr,
+    ld, ss, rs, out_s, in_s,
 ):
     a = lax.axis_index("attn")
     f = lax.axis_index("ffn")
@@ -85,17 +85,28 @@
         return cp
 
     sent = []
-
-    def send(src, dst, dev, arrival=None):
-        k = len(sent)
-        cp = pltpu.make_async_remote_copy(
-            src_ref=src, dst_ref=dst, send_sem=ss.at[k],
-            recv_sem=rs.at[k] if arrival is None else arrival,
+    groups = {}
+
+    def remote(src, dst, send_sem, recv_sem, dev):
+        return pltpu.make_async_remote_copy(
+            src_ref=src, dst_ref=dst, send_sem=send_sem, recv_sem=recv_sem,
             device_id=dev, device_id_type=MESH,
         )
+
+    def send(src, dst, dev, group=None, arrival=None):
+        k = len(sent)
+        if group is None:
+            leave = ss.at[k]
+        else:
+            groups[group] = groups.get(group, 0) + 1
+            leave = out_s.at[group]
+        cp = remote(src, dst, leave, rs.at[k] if arrival is None else in_s.at[arrival], dev)
         cp.start()
-        sent.append(cp)
+        sent.append((group, cp))
         return cp
+
+    def wait_in(blocks, arrival):
+        remote(blocks, blocks, out_s.at[0], in_s.at[arrival], sib).wait_recv()
 
     l_q = load(q_h.at[0], qv)
     l_k = load(k_h.at[0], kv)
@@ -150,18 +161,19 @@
     x_wu = send(wu_h.at[1 - c], wu.at[c, pl.ds(0, W)], sib)
     x_wd = send(wd_h.at[1 - c], wd.at[c, pl.ds(0, W)], sib)
 
-    def gather_z(buf):
+    def gather_z(buf, group):
         got = {}
 
         def pass_on(o):
             block = buf.at[zidx(-o)]
             for to in RELAY[abs(o)]:
                 if o == 0:
-                    got[to] = send(block, block, zdev(to))
-                    got[-to] = send(block, block, zdev(-to))
+                    got[to] = send(block, block, zdev(to), group)
+                    got[-to] = send(block, block, zdev(-to), group)
                 elif to < 8:
                     sgn = 1 if o > 0 else -1
-                    got[sgn * to] = send(block, block, zdev(sgn * to - o))
+                    arrival = 2 * group + (sgn * to in LAST)
+                    send(block, block, zdev(sgn * to - o), group, arrival)
 
         pass_on(0)
         yield
@@ -172,19 +184,17 @@
         got[5].wait_recv()
         got[-5].wait_recv()
         far = buf.at[zidx(-5 * sg)]
-        got[8] = send(far, far, zdev(3 * sg))
+        send(far, far, zdev(3 * sg), group, 2 * group + 1)
         pass_on(5)
         pass_on(-5)
         yield
-        for o in MIDDLE[2:]:
-            got[o].wait_recv()
+        wait_in(buf.at[pl.ds(0, len(MIDDLE) - 2)], 2 * group)
         yield
-        for o in LAST:
-            got[o].wait_recv()
+        wait_in(buf.at[pl.ds(0, len(LAST))], 2 * group + 1)
 
     x_cp.wait_recv()
     ag1[z] = jnp.where(mine, att[c], 0.0).astype(BF) + xr[...]
-    heads = gather_z(ag1)
+    heads = gather_z(ag1, 0)
     next(heads)
 
     for buf in (wo, wg, wu, wd):
@@ -232,15 +242,13 @@
         p1 = mm(rows, wo[s, :, 1024:2048], NT).reshape(CHIPS, 16, WP)
         u = p0[:, 0:8] + p1[:, 8:16]
         us[s] = u.reshape(4, ROWS, WP).astype(BF)
-    pending = []
     for df, dc in XCORE:
         q = lax.rem(f + df, 4)
         s = lax.rem(c + dc, 2)
-        pending.append(send(us.at[s, q], rb.at[f * 2 + c], pdev((df, 0, dc))))
+        send(us.at[s, q], rb.at[f * 2 + c], pdev((df, 0, dc)), 3, 6)
     rb[f * 2 + c] = us[c, f]
     hidden = pad32[...]
-    for cp in pending:
-        cp.wait_recv()
+    wait_in(rb.at[pl.ds(0, 7)], 6)
     for k in range(8):
         hidden = hidden + rb[k].astype(F32)
     hid = hidden.astype(BF).astype(F32)
@@ -252,19 +260,17 @@
     ).astype(BF)
     tok[...] = mm(pick, normed).astype(BF).reshape(8, SLOT, WP)
 
-    pending = []
     for o in PLANE:
         e = lax.rem(f + o[0], 4) * 2 + lax.rem(c + o[2], 2)
-        pending.append(send(tok.at[e], xb.at[c, r * 4 + f], pdev(o)))
-    xb[c, r * 4 + f] = tok[f * 2 + c]
+        send(tok.at[e], xb.at[c * 16 + r * 4 + f], pdev(o), 4, 7)
+    xb[c * 16 + r * 4 + f] = tok[f * 2 + c]
     l_wg.wait()
     x_wg.wait_recv()
     l_wu.wait()
     x_wu.wait_recv()
-    for cp in pending:
-        cp.wait_recv()
-    x0 = xb[0].reshape(256, WP)
-    x1 = xb[1].reshape(256, WP)
+    wait_in(xb.at[pl.ds(0, 31)], 7)
+    x0 = xb[0:16].reshape(256, WP)
+    x1 = xb[16:32].reshape(256, WP)
     ones = lax.broadcasted_iota(jnp.int32, (16, WP), 1)
     ones = jnp.where((ones == W) | (ones == W + 1), 1.0, 0.0).astype(BF)
     sq = (mm(ones, x0, NT) + mm(ones, x1, NT))[0:1, :]
@@ -294,52 +300,51 @@
     sides = ((0, 1), (1, -1))
 
     class Sum:
-        def __init__(self, pb, r1, ra, s2, r2):
-            self.pb, self.r1, self.ra, self.s2, self.r2 = pb, r1, ra, s2, r2
-            self.leaf, self.ends = {}, []
+        def __init__(self, pb, r1, s2, r2, group):
+            self.pb, self.r1, self.s2, self.r2 = pb, r1, s2, r2
+            self.group, self.arrival = group, 8 + 3 * (group - 5)
 
         def leaves(self):
-            for k, (o, d) in enumerate(((7, -1), (5, 1), (4, -2), (3, -1), (1, 1))):
+            slots = ((7, -1, 0), (5, 1, 2), (8, 0, 4), (4, -2, 5), (3, -1, 7), (1, 1, 9))
+            for o, d, k in slots:
+                arrival = self.arrival + (k > 4)
+                if o == 8:
+                    send(self.pb.at[zidx(8)], self.r1.at[k], zdev(-2 * sg), self.group, arrival)
+                    continue
                 for side, sgn in sides:
                     src = self.pb.at[zidx(-sgn * o)]
-                    self.leaf[side, k] = send(src, self.r1.at[side, k], zdev(sgn * d))
-                if o == 5:
-                    self.anti = send(self.pb.at[zidx(8)], self.ra, zdev(-2 * sg))
-
-        def relay(self, slot, o, parts):
+                    send(src, self.r1.at[k + side], zdev(sgn * d), self.group, arrival)
+
+        def relay(self, slot, o, first, last):
+            wait_in(self.r1.at[pl.ds(first, last - first)], self.arrival + slot)
             for side, sgn in sides:
                 acc = self.pb[zidx(-sgn * o)].astype(F32)
-                for k in parts:
-                    self.leaf[side, k].wait_recv()
-                    acc = acc + self.r1[side, k].astype(F32)
+                for k in range(first + side, min(last, first + 4) if o == 6 else last, 2):
+                    acc = acc + self.r1[k].astype(F32)
                 if o == 6:
-                    if side == 0:
-                        self.anti.wait_recv()
-                    acc = acc + jnp.where(c == side, self.ra[...].astype(F32), 0.0)
-                self.s2[side, slot] = acc.astype(BF)
-                src = self.s2.at[side, slot]
-                self.ends.append(send(src, self.r2.at[side, slot], zdev(-sgn * o)))
+                    acc = acc + jnp.where(c == side, self.r1[4].astype(F32), 0.0)
+                k = 2 * slot + side
+                self.s2[k] = acc.astype(BF)
+                send(self.s2.at[k], self.r2.at[k], zdev(-sgn * o), self.group, self.arrival + 2)
 
         def total(self):
+            wait_in(self.r2, self.arrival + 2)
             out = self.pb[z].astype(F32)
-            for cp in self.ends:
-                cp.wait_recv()
-            for side in range(2):
-                for k in range(2):
-                    out = out + self.r2[side, k].astype(F32)
+            for k in range(4):
+                out = out + self.r2[k].astype(F32)
             return out
 
-    sum_a, sum_b = Sum(pb_a, r1_a, ra_a, s2_a, r2_a), Sum(pb_b, r1_b, ra_b, s2_b, r2_b)
+    sum_a, sum_b = Sum(pb_a, r1_a, s2_a, r2_a, 5), Sum(pb_b, r1_b, s2_b, r2_b, 6)
     put(pb_a, 0, project(wg, 0, EA), 0)
     put(pb_a, EA, project(wu, 0, EA), 3)
     sum_a.leaves()
     put(pb_b, 0, project(wg, EA, EFF), 6)
     put(pb_b, EB, project(wu, EA, TAIL), 8)
     sum_b.leaves()
-    sum_a.relay(0, 6, (0, 1))
-    sum_b.relay(0, 6, (0, 1))
-    sum_a.relay(1, 2, (2, 3, 4))
-    sum_b.relay(1, 2, (2, 3, 4))
+    sum_a.relay(0, 6, 0, 5)
+    sum_b.relay(0, 6, 0, 5)
+    sum_a.relay(1, 2, 5, 11)
+    sum_b.relay(1, 2, 5, 11)
 
     def activate(gate, up):
         gate, up = gate * rinv, up * rinv
@@ -358,7 +363,7 @@
     sq = jnp.sum(jnp.where(lane3 == z * SLOT + row, sq, 0.0), axis=1, keepdims=True)
     rinv = lax.rsqrt(sq / D + 1e-6)
     ag2_a[z] = activate(total[:, 0:EA], total[:, EA : 2 * EA])
-    rows_a = gather_z(ag2_a)
+    rows_a = gather_z(ag2_a, 1)
     next(rows_a)
     total = sum_b.total()
     for t in range(3):
@@ -367,7 +372,7 @@
     last_up[CAP:SLOT, :] = jnp.zeros((SLOT - CAP, 128), F32)
     up = jnp.concatenate([total[:, EB : EB + 128], last_up[...]], axis=1)
     ag2_b[z] = activate(total[:, 0:EB], up)
-    rows_b = gather_z(ag2_b)
+    rows_b = gather_z(ag2_b, 2)
     next(rows_b)
 
     l_wd.wait()
@@ -386,17 +391,15 @@
             b = zidx(-o)
             fo, ro = lax.rem(b, 4), lax.div(b, 4)
             i = first + k
-            send(eb.at[1 - c, i], rr.at[me], {"attn": z * 2 + 1 - c, "ffn": fo, "rep": ro}, back_s.at[me])
-            cp = pltpu.make_async_remote_copy(
-                src_ref=eb.at[c, i], dst_ref=rr.at[me], send_sem=stay_s.at[i],
-                recv_sem=back_s.at[me], device_id={"ffn": fo, "rep": ro}, device_id_type=MESH,
-            )
+            stay.append(i)
+            dev = {"attn": z * 2 + 1 - c, "ffn": fo, "rep": ro}
+            send(eb.at[1 - c, i], rr.at[me], dev, 7, 14)
             away = b != r * 4 + f
-            stay.append((away, cp))
 
             @pl.when(away)
             def _():
-                cp.start()
+                dev = {"attn": z * 2 + c, "ffn": fo, "rep": ro}
+                remote(eb.at[c, i], rr.at[me], out_s.at[7], in_s.at[14], dev).start()
 
             @pl.when(jnp.logical_not(away))
             def _():
@@ -414,21 +417,18 @@
         for _ in rows:
             pass
     give_back(LAST)
-    for j in range(1, 32):
-        k = lax.rem(me + j, 32)
-        pltpu.make_async_remote_copy(
-            src_ref=eb.at[0, 0], dst_ref=rr.at[k], send_sem=stay_s.at[0],
-            recv_sem=back_s.at[k], device_id=sib, device_id_type=MESH,
-        ).wait_recv()
+    wait_in(rr.at[pl.ds(0, 31)], 14)
     back = rr[...].reshape(512, WP)
     mixed = hidden + mm(share_hi, back) + mm(share_lo, back)
     out_ref[0] = mixed[:, 0:W]
-    for cp in sent:
-        cp.wait_send()
-    for away, cp in stay:
-        @pl.when(away)
-        def _():
+    for group, cp in sent:
+        if group is None:
             cp.wait_send()
+    groups[7] = 31
+    whole = {0: ag1, 1: ag2_a, 2: ag2_b, 3: rb, 4: xb, 5: pb_a, 6: pb_b, 7: rr}
+    for group, n in groups.items():
+        blocks = whole[group].at[pl.ds(0, n)]
+        remote(blocks, blocks, out_s.at[group], in_s.at[0], sib).wait_send()
 
 
 N_SENT = 5 + 15 + 7 + 31 + 30 + 30 + 16
@@ -469,17 +469,15 @@
             vm((ROWS, WP), F32),
             vm((1, WP), F32),
             vm((8, SLOT, WP), BF),
-            vm((2, 16, SLOT, WP), BF),
+            vm((32, SLOT, WP), BF),
             vm((CHIPS, SLOT, 2 * EA), BF),
-            vm((2, 5, SLOT, 2 * EA), BF),
-            vm((SLOT, 2 * EA), BF),
-            vm((2, 2, SLOT, 2 * EA), BF),
-            vm((2, 2, SLOT, 2 * EA), BF),
+            vm((11, SLOT, 2 * EA), BF),
+            vm((4, SLOT, 2 * EA), BF),
+            vm((4, SLOT, 2 * EA), BF),
             vm((CHIPS, SLOT, EB + 128), BF),
-            vm((2, 5, SLOT, EB + 128), BF),
-            vm((SLOT, EB + 128), BF),
-            vm((2, 2, SLOT, EB + 128), BF),
-            vm((2, 2, SLOT, EB + 128), BF),
+            vm((11, SLOT, EB + 128), BF),
+            vm((4, SLOT, EB + 128), BF),
+            vm((4, SLOT, EB + 128), BF),
             vm((SLOT, 128), F32),
             vm((CHIPS, SLOT, EA), BF),
             vm((CHIPS, SLOT, EB), BF),
@@ -488,8 +486,8 @@
             dma((12,)),
             dma((N_SENT,)),
             dma((N_SENT,)),
-            dma((16,)),
-            dma((32,)),
+            dma((8,)),
+            dma((15,)),
         ],
         compiler_params=pltpu.CompilerParams(
             collective_id=0, has_side_effects=True, vmem_limit_bytes=56 * 1024 * 1024

time: 77.1 us -> 76.6 us (level)
  no operation moved by 1% of the time
where the time goes in v4:
time: 76.6 us; the launch traced here: 76.4 us
  Pallas kernels  75.8 us (99%)
    pallas_call x1, Pallas kernels, per_device(): pl.pallas_call(kernel, name='layer', out_shape=pltpu.VMEM((1, ROWS, W), F...  75.8 us

profile of v4, /device:TPU:16, one launch (start us, length us, event | category | flops | bytes accessed | tf_op | source)
XLA Modules:
  0.0 76.4 jit_solution(5253499671307038844)
XLA Ops:
  0.0 75.8 %layer.1 = f32[1,32,224]{2,1,0:T(8,128)S(1)} custom-call(bf16[1,4,4096]{2,1,0:T(4,128)(2,1)} %q_h.1, bf16[1,4,256,256]{3,2,1,0:T(8,128)(2,1)} %k_h.1, bf16[1,4,256,256]{3,2,1,0:T(8,128)(2,1)} %v_h.1, s32[1,4]{1,0:T(1,128)} %len_h.1, bf16[224,4096]{1,0:T(8,128)(2,1)} %wo_h.1, bf16[1,32,224]{2,1,0:T(8,128)(2,1)} %res_h.1, f32[1,224]{1,0:T(1,128)} %bitcast.5, ...), custom_call_target="tpu_custom_call" | custom-call | tf_op jit(solution)/shard_map/layer/pallas_call | solution.py:443
  75.8 0.6 copy.14

commit v5 on v4

--- a/solution.py
+++ b/solution.py
@@ -50,7 +50,7 @@
     q_h, k_h, v_h, len_h, wo_h, res_h, gain_h, ids_h, gw_h, wg_h, wu_h, wd_h,
     out_ref,
     qv, kv, vv, lenv, resv, gainv, idsv, gwv, wo, wg, wu, wd,
-    qs, att, xs, xr, ag1, us, rb, pad32, pad1, tok, xb, pb_a, r1_a, s2_a, r2_a, pb_b, r1_b, s2_b, r2_b, last_up, ag2_a, ag2_b, eb, rr,
+    qs, att, xs, xr, ag1, ag1b, us, rb, pad32, pad1, tok, xb, pb_a, r1_a, s2_a, r2_a, pb_b, r1_b, s2_b, r2_b, last_up, ag2_a, ag2_b, eb, rr,
     ld, ss, rs, out_s, in_s,
 ):
     a = lax.axis_index("attn")
@@ -193,9 +193,13 @@
         wait_in(buf.at[pl.ds(0, len(LAST))], 2 * group + 1)
 
     x_cp.wait_recv()
-    ag1[z] = jnp.where(mine, att[c], 0.0).astype(BF) + xr[...]
+    whole_block = jnp.where(mine, att[c], 0.0).astype(BF) + xr[...]
+    ag1[z] = whole_block[:, 0:512]
+    ag1b[z] = whole_block[:, 512:1024]
     heads = gather_z(ag1, 0)
+    heads_b = gather_z(ag1b, 8)
     next(heads)
+    next(heads_b)
 
     for buf in (wo, wg, wu, wd):
         buf[:, W:WP, :] = jnp.zeros((2, WP - W, buf.shape[2]), BF)
@@ -231,15 +235,21 @@
     share_lo = jnp.concatenate([mm(eye, share_lo, NT).astype(BF)] * 4, axis=1)
 
 
-    for _ in heads:
-        pass
+    for _ in range(2):
+        next(heads)
+        next(heads_b)
+    for it in (heads, heads_b):
+        for _ in it:
+            pass
     l_wo.wait()
     x_wo.wait_recv()
 
-    rows = ag1[...].reshape(CHIPS * 16, 1024)
+    rows = ag1[...].reshape(CHIPS * 16, 512)
+    rows_b = ag1b[...].reshape(CHIPS * 16, 512)
     for s in range(2):
-        p0 = mm(rows, wo[s, :, 0:1024], NT).reshape(CHIPS, 16, WP)
-        p1 = mm(rows, wo[s, :, 1024:2048], NT).reshape(CHIPS, 16, WP)
+        p0 = mm(rows, wo[s, :, 0:512], NT) + mm(rows_b, wo[s, :, 512:1024], NT)
+        p1 = mm(rows, wo[s, :, 1024:1536], NT) + mm(rows_b, wo[s, :, 1536:2048], NT)
+        p0, p1 = p0.reshape(CHIPS, 16, WP), p1.reshape(CHIPS, 16, WP)
         u = p0[:, 0:8] + p1[:, 8:16]
         us[s] = u.reshape(4, ROWS, WP).astype(BF)
     for df, dc in XCORE:
@@ -425,13 +435,13 @@
         if group is None:
             cp.wait_send()
     groups[7] = 31
-    whole = {0: ag1, 1: ag2_a, 2: ag2_b, 3: rb, 4: xb, 5: pb_a, 6: pb_b, 7: rr}
+    whole = {8: ag1b, 0: ag1, 1: ag2_a, 2: ag2_b, 3: rb, 4: xb, 5: pb_a, 6: pb_b, 7: rr}
     for group, n in groups.items():
         blocks = whole[group].at[pl.ds(0, n)]
         remote(blocks, blocks, out_s.at[group], in_s.at[0], sib).wait_send()
 
 
-N_SENT = 5 + 15 + 7 + 31 + 30 + 30 + 16
+N_SENT = 5 + 30 + 7 + 31 + 30 + 30 + 16
 
 
 def per_device(q, k, v, lens, wo, res, gain, ids, gw, wg, wu, wd):
@@ -463,7 +473,8 @@
             vm((2, 16, 1024), F32),
             vm((16, 1024), BF),
             vm((16, 1024), BF),
-            vm((CHIPS, 16, 1024), BF),
+            vm((CHIPS, 16, 512), BF),
+            vm((CHIPS, 16, 512), BF),
             vm((2, 4, ROWS, WP), BF),
             vm((8, ROWS, WP), BF),
             vm((ROWS, WP), F32),
@@ -486,8 +497,8 @@
             dma((12,)),
             dma((N_SENT,)),
             dma((N_SENT,)),
-            dma((8,)),
-            dma((15,)),
+            dma((9,)),
+            dma((18,)),
         ],
         compiler_params=pltpu.CompilerParams(
             collective_id=0, has_side_effects=True, vmem_limit_bytes=56 * 1024 * 1024

time: 76.6 us -> 74.9 us (0.978)
  Pallas kernels: 75.8 us -> 74.1 us
    pallas_call x1, Pallas kernels: 75.8 us -> 74.1 us  [per_device(): pl.pallas_call(kernel, name='layer', out_shape=pltpu.VMEM((1, ROWS, W), F...]
where the time goes in v5:
time: 74.9 us; the launch traced here: 74.7 us
  Pallas kernels  74.1 us (99%)
    pallas_call x1, Pallas kernels, per_device(): pl.pallas_call(kernel, name='layer', out_shape=pltpu.VMEM((1, ROWS, W), F...  74.1 us

profile of v5, /device:TPU:16, one launch (start us, length us, event | category | flops | bytes accessed | tf_op | source)
XLA Modules:
  0.0 74.7 jit_solution(4549264778391438101)
XLA Ops:
  0.0 74.1 %layer.1 = f32[1,32,224]{2,1,0:T(8,128)S(1)} custom-call(bf16[1,4,4096]{2,1,0:T(4,128)(2,1)} %q_h.1, bf16[1,4,256,256]{3,2,1,0:T(8,128)(2,1)} %k_h.1, bf16[1,4,256,256]{3,2,1,0:T(8,128)(2,1)} %v_h.1, s32[1,4]{1,0:T(1,128)} %len_h.1, bf16[224,4096]{1,0:T(8,128)(2,1)} %wo_h.1, bf16[1,32,224]{2,1,0:T(8,128)(2,1)} %res_h.1, f32[1,224]{1,0:T(1,128)} %bitcast.5, ...), custom_call_target="tpu_custom_call" | custom-call | tf_op jit(solution)/shard_map/layer/pallas_call | solution.py:453
  74.1 0.6 copy.14

commit v6 on v5

--- a/solution.py
+++ b/solution.py
@@ -156,10 +156,6 @@
 
     pl.semaphore_wait(barrier, len(peers))
     x_cp = send(xs, xr, sib)
-    x_wo = send(wo_h.at[:, pl.ds(other, KH)], wo.at[c, pl.ds(0, W)], sib)
-    x_wg = send(wg_h.at[1 - c], wg.at[c, pl.ds(0, W)], sib)
-    x_wu = send(wu_h.at[1 - c], wu.at[c, pl.ds(0, W)], sib)
-    x_wd = send(wd_h.at[1 - c], wd.at[c, pl.ds(0, W)], sib)
 
     def gather_z(buf, group):
         got = {}
@@ -200,6 +196,10 @@
     heads_b = gather_z(ag1b, 8)
     next(heads)
     next(heads_b)
+    x_wo = send(wo_h.at[:, pl.ds(other, KH)], wo.at[c, pl.ds(0, W)], sib)
+    x_wg = send(wg_h.at[1 - c], wg.at[c, pl.ds(0, W)], sib)
+    x_wu = send(wu_h.at[1 - c], wu.at[c, pl.ds(0, W)], sib)
+    x_wd = send(wd_h.at[1 - c], wd.at[c, pl.ds(0, W)], sib)
 
     for buf in (wo, wg, wu, wd):
         buf[:, W:WP, :] = jnp.zeros((2, WP - W, buf.shape[2]), BF)

time: 74.9 us -> 75 us (level)
  no operation moved by 1% of the time
where the time goes in v6:
time: 75 us; the launch traced here: 74.8 us
  Pallas kernels  74.2 us (99%)
    pallas_call x1, Pallas kernels, per_device(): pl.pallas_call(kernel, name='layer', out_shape=pltpu.VMEM((1, ROWS, W), F...  74.2 us

profile of v6, /device:TPU:16, one launch (start us, length us, event | category | flops | bytes accessed | tf_op | source)
XLA Modules:
  0.0 74.8 jit_solution(9039875001198650691)
XLA Ops:
  0.0 74.2 %layer.1 = f32[1,32,224]{2,1,0:T(8,128)S(1)} custom-call(bf16[1,4,4096]{2,1,0:T(4,128)(2,1)} %q_h.1, bf16[1,4,256,256]{3,2,1,0:T(8,128)(2,1)} %k_h.1, bf16[1,4,256,256]{3,2,1,0:T(8,128)(2,1)} %v_h.1, s32[1,4]{1,0:T(1,128)} %len_h.1, bf16[224,4096]{1,0:T(8,128)(2,1)} %wo_h.1, bf16[1,32,224]{2,1,0:T(8,128)(2,1)} %res_h.1, f32[1,224]{1,0:T(1,128)} %bitcast.5, ...), custom_call_target="tpu_custom_call" | custom-call | tf_op jit(solution)/shard_map/layer/pallas_call | solution.py:453
  74.2 0.6 copy.14
